TPU v7x, 32 devices: a whole 2x2x4 slice. The times are simulated.
32 devices in a mesh: quad: 16 (over z, x, core), rows: 2 (over y).
Axes of the slice: x: 2, y: 2, z: 4, core: 2. Of those that a mesh axis runs over, the one named last changes fastest.
Arguments:
- solutions: bfloat16 [32, 2, 64, 16, 1280], P('quad', None, None, None, 'rows'), may hold values from -64 to 64
- angles: float32 [32], replicated, may hold values from -3.140625 to 3.140625
- qweights: float32 [2, 32], replicated, may hold values from -1 to 1
- neighbours: int32 [320, 8], P(('quad', 'rows')), may hold values from 0 to 319, as said below
- hblocks: bfloat16 [320, 64, 512], P(('quad', 'rows')), may hold values from -0.25 to 0.25
Outputs:
- h_moments: bfloat16 [1024, 20480], P(None, ('quad', 'rows'))
- ritz_matrices: float32 [512, 2, 2, 512], P('quad')
Inputs may be any that keep to these rules, and one draw needn't show every extreme that they name: neighbours[c, 0] = c, neighbours[c, 1] = min(c + 2, 319), neighbours[c, 2] = max(c - 2, 0); every entry lies within 2 of c.
All inputs are finite; a program needn't handle non-finite values.
Results may differ from a plain program's by a relative error of at most 0.0075.
Values may be sent and summed in bfloat16 or wider, within the bound.
A program may use at most 64 MiB of HBM per device.

v0:
```python
import jax
import jax.numpy as jnp
from jax import lax
from jax.sharding import PartitionSpec as P

LCOL = 64
QPTS = 32
KMOM = 8
NB = 8
HALO = 2


def extended(block, sides, width):
    for axis, dim in sides:
        count = lax.axis_size(axis)
        forward = [(i, i + 1) for i in range(count - 1)]
        backward = [(target, source) for source, target in forward]
        low = lax.ppermute(
            lax.slice_in_dim(block, block.shape[dim] - width, None, axis=dim), axis, forward
        )
        high = lax.ppermute(lax.slice_in_dim(block, 0, width, axis=dim), axis, backward)
        block = jnp.concatenate([low, block, high], axis=dim)
    return block


def moment_coefficients(angles, qweights):
    order = jnp.arange(KMOM, dtype=jnp.float32)[:, None]
    phase = order * angles[None, :]
    cosine = jnp.cos(phase)
    sine = jnp.sin(phase)
    real_coef = qweights[0][None, :] * cosine - qweights[1][None, :] * sine
    imag_coef = qweights[0][None, :] * sine + qweights[1][None, :] * cosine
    real_rows = jnp.stack([real_coef, -imag_coef], -1)
    imag_rows = jnp.stack([imag_coef, real_coef], -1)
    mixing = jnp.stack([real_rows, imag_rows], 0)
    return mixing.reshape(2 * KMOM, 2 * QPTS).astype(jnp.bfloat16)


def split_parts(product, half_cols, row_count):
    real_part = product[:row_count, :half_cols] + product[row_count:, half_cols:]
    imag_part = product[:row_count, half_cols:] - product[row_count:, :half_cols]
    return jnp.stack([real_part, imag_part], 1)


def gram_part(moments, applied, first_row, row_count, total_rows):
    half_cols = moments.shape[0] // 2
    chosen = jnp.concatenate(
        [
            lax.dynamic_slice_in_dim(moments, first_row, row_count, 0),
            lax.dynamic_slice_in_dim(moments, half_cols + first_row, row_count, 0),
        ],
        0,
    )
    contract = (((1,), (1,)), ((), ()))
    plain = lax.dot_general(chosen, moments, contract, preferred_element_type=jnp.float32)
    mixed = lax.dot_general(chosen, applied, contract, preferred_element_type=jnp.float32)
    ritz = jnp.stack(
        [split_parts(plain, half_cols, row_count), split_parts(mixed, half_cols, row_count)], 1
    )
    return ritz * (1.0 / total_rows)


def per_device(solutions, angles, qweights, neighbours, hblocks):
    groups = lax.axis_size("quad") * lax.axis_size("rows")
    rows_dev = solutions.shape[4]
    cells_dev = hblocks.shape[0]
    orbitals = hblocks.shape[1]
    half_cols = KMOM * LCOL
    mixing = moment_coefficients(angles, qweights)
    received = lax.all_to_all(solutions, "quad", split_axis=3, concat_axis=0, tiled=True)
    stacked = received.reshape(QPTS * 2, LCOL, received.shape[4])
    result = jnp.einsum("pq,qln->pln", mixing, stacked, preferred_element_type=jnp.float32)
    moments = result.reshape(2 * half_cols, received.shape[4]).astype(jnp.bfloat16)
    padded = extended(moments, ((("quad", "rows"), 1),), HALO * orbitals)
    first_cell = (
        lax.axis_index("quad") * lax.axis_size("rows") + lax.axis_index("rows")
    ) * cells_dev
    local_index = (neighbours - first_cell + HALO).reshape(-1)
    cellwise = padded.reshape(2 * half_cols, cells_dev + 2 * HALO, orbitals)
    nearby = jnp.take(cellwise, local_index, axis=1).reshape(
        2 * half_cols, cells_dev, NB * orbitals
    )
    applied = jnp.einsum("cam,xcm->xca", hblocks, nearby, preferred_element_type=jnp.float32)
    applied = applied.reshape(2 * half_cols, rows_dev).astype(jnp.bfloat16)
    total_rows = rows_dev * groups
    share_rows = half_cols // lax.axis_size("quad")
    summed = lax.psum(gram_part(moments, applied, 0, half_cols, total_rows), ("quad", "rows"))
    ritz_matrices = lax.dynamic_slice_in_dim(
        summed, lax.axis_index("quad") * share_rows, share_rows, 0
    )
    return (applied, ritz_matrices)


def solution(mesh):
    in_specs = (
        P("quad", None, None, None, "rows"),
        P(),
        P(),
        P(("quad", "rows"), None),
        P(("quad", "rows"), None, None),
    )
    out_specs = (P(None, ("quad", "rows")), P("quad", None, None, None))
    return jax.shard_map(
        per_device, mesh=mesh, in_specs=in_specs, out_specs=out_specs, check_vma=False
    )
```

profile of v0, /device:TPU:0, one launch (start us, length us, event | category | flops | bytes accessed | tf_op | source)
XLA Modules:
  0.0 333.4 jit_solution(11366127904357081607)
XLA Ops:
  7.2 6.2 %copy.34 = bf16[2,2,64,16,640]{4,2,1,0,3:T(8,128)(2,1)} copy(bf16[2,2,64,16,640]{4,3,2,1,0:T(8,128)(2,1)} %param.5) | data formatting | bytes 10485760 | tf_op args[0]
  13.3 7.5 %all-to-all-start = ((bf16[2,2,64,16,640]{4,2,1,0,3:T(8,128)(2,1)}), bf16[2,2,64,16,640]{4,2,1,0,3:T(8,128)(2,1)}, u32[]{:S(2)}, u32[]{:S(2)}) async-start(bf16[2,2,64,16,640]{4,2,1,0,3:T(8,128)(2,1)} %copy.34), calls=%async_computation | async-start | bytes 10485760 | tf_op jit(solution)/shard_map/all_to_all | solution.py:70
  21.0 0.1 negate_convert_fusion
  21.0 0.1 copy.33
  21.2 0.1 convert_element_type.30
  21.3 0.1 copy.39
  21.4 0.1 reshape.334
  21.5 0.1 copy.32
  21.6 0.1 broadcast_in_dim.16
  21.6 0.1 broadcast_in_dim.17
  21.8 95.1 %all-to-all-done = bf16[2,2,64,16,640]{4,2,1,0,3:T(8,128)(2,1)} async-done(((bf16[2,2,64,16,640]{4,2,1,0,3:T(8,128)(2,1)}), bf16[2,2,64,16,640]{4,2,1,0,3:T(8,128)(2,1)}, u32[]{:S(2)}, u32[]{:S(2)}) %all-to-all-start) | async-done | bytes 5242912 | tf_op jit(solution)/shard_map/all_to_all | solution.py:70
  116.8 6.5 %fusion.6 = bf16[16,64,640]{2,0,1:T(8,128)(2,1)S(1)} fusion(bf16[64,64,640]{2,1,0:T(8,128)(2,1)} %bitcast.7, bf16[16,64]{0,1:T(8,128)(2,1)S(1)} %convert_element_type.30), kind=kOutput, calls=%fused_computation.11 | convolution fusion | flops 84541440 | bytes 6555648 | tf_op jit(solution)/shard_map/pq,qln->pln/dot_general | solution.py:72
  123.3 0.3 copy.37
  123.7 1.8 fusion.23
  125.5 3.4 %collective-permute-start = (bf16[1024,128]{1,0:T(8,128)(2,1)S(1)}, bf16[1024,128]{1,0:T(8,128)(2,1)S(1)}, u32[]{:S(2)}, u32[]{:S(2)}) collective-permute-start(bf16[1024,128]{1,0:T(8,128)(2,1)S(1)} %get-tuple-element.14), channel_id=1, source_target_pairs={{0,1},{1,2},{2,3},{3,4},{4,5},{5,6},{6,7},{7,8},{8,9},{9,10},{10,1... | collective-permute-start | bytes 786440 | tf_op jit(solution)/shard_map/ppermute | solution.py:18
  128.9 1.5 collective-permute-start.1
  130.4 1.5 fusion.15
  131.9 3.7 %collective-permute-done = bf16[1024,128]{1,0:T(8,128)(2,1)S(1)} collective-permute-done((bf16[1024,128]{1,0:T(8,128)(2,1)S(1)}, bf16[1024,128]{1,0:T(8,128)(2,1)S(1)}, u32[]{:S(2)}, u32[]{:S(2)}) %collective-permute-start) | collective-permute-done | bytes 262176 | tf_op jit(solution)/shard_map/ppermute | solution.py:18
  135.6 1.6 collective-permute-done.1
  137.2 1.4 pad_maximum_fusion
  138.6 2.9 copy.38
  141.5 6.3 %gather_fusion = bf16[80,1024,64]{1,2,0:T(8,128)(2,1)} fusion(bf16[1024,14,64]{0,2,1:T(8,128)(2,1)S(1)} %bitcast.45, s32[1024]{0:T(1024)S(1)} %pad_clamp_fusion), kind=kCustom, calls=%fused_computation | custom fusion | bytes 20971840 | tf_op jit(solution)/shard_map/jit(_take)/gather | solution.py:80
  147.9 5.5 %fusion.9 = bf16[10,1024,64]{1,2,0:T(8,128)(2,1)S(1)} fusion(bf16[10,64,512]{2,1,0:T(8,128)(2,1)S(1)} %copy-done, bf16[1024,10,512]{0,2,1:T(8,128)(2,1)} %bitcast.46, pred[10,512]{1,0:T(8,128)(4,1)S(1)} %broadcast_in_dim.17), kind=kOutput, calls=%fused_computation.12 | convolution fusion | flops 676986880 | bytes 12456960 | tf_op jit(solution)/shard_map/cam,xcm->xca/dot_general | solution.py:83
  153.4 1.8 fusion.24
  155.2 0.5 fusion.13
  155.7 0.7 copy-done.3
  156.4 0.4 maximum_bitcast_fusion
  156.9 2.7 maximum_multiply_fusion
  159.7 1.4 copy.41
  161.1 163.6 %all-reduce.2.cloned.1.call-done = f32[512,2,2,512]{3,0,2,1:T(8,128)} async-done(((f32[512,2,2,512]{3,0,2,1:T(8,128)}), f32[512,2,2,512]{3,0,2,1:T(8,128)}) %all-reduce.2.cloned.1.call-update) | async-done | bytes 4194320 | tf_op jit(solution)/shard_map/psum | solution.py:87
  324.7 1.0 constant_dynamic-slice_fusion
  325.6 0.9 copy.42
  (23 shorter events, 0.2 us)
Async XLA Ops:
  7.2 140.7 %copy-start = (bf16[10,64,512]{2,1,0:T(8,128)(2,1)S(1)}, bf16[10,64,512]{2,1,0:T(8,128)(2,1)}, u32[]{:S(2)}) copy-start(bf16[10,64,512]{2,1,0:T(8,128)(2,1)} %param.9) | copy-start | bytes 1966084
  13.3 7.6 %copy-start.5 = (f32[2,32]{1,0:T(2,128)S(1)}, f32[2,32]{1,0:T(2,128)}, u32[]{:S(2)}) copy-start(f32[2,32]{1,0:T(2,128)} %param.7) | copy-start | bytes 772
  13.3 7.6 %copy-start.6 = (f32[32]{0:T(128)S(1)}, f32[32]{0:T(128)}, u32[]{:S(2)}) copy-start(f32[32]{0:T(128)} %param.6) | copy-start | bytes 388
  13.3 7.9 %copy-start.4 = (s32[10,8]{0,1:T(8,128)S(1)}, s32[10,8]{0,1:T(8,128)}, u32[]{:S(2)}) copy-start(s32[10,8]{0,1:T(8,128)} %param.8) | copy-start | bytes 964
  13.3 103.5 %all-to-all-start = ((bf16[2,2,64,16,640]{4,2,1,0,3:T(8,128)(2,1)}), bf16[2,2,64,16,640]{4,2,1,0,3:T(8,128)(2,1)}, u32[]{:S(2)}, u32[]{:S(2)}) async-start(bf16[2,2,64,16,640]{4,2,1,0,3:T(8,128)(2,1)} %copy.34), calls=%async_computation | async-start | bytes 10485760 | tf_op jit(solution)/shard_map/all_to_all | solution.py:70
  20.9 303.8 %all-reduce.2.cloned.1.call-start = ((), (), s32[]{:S(2)}) async-start(), calls=%async_computation.1 | async-start | bytes 8388608 | tf_op jit(solution)/shard_map/psum | solution.py:87
  123.6 13.6 %copy-start.1 = (bf16[16,64,640]{2,1,0:T(8,128)(2,1)}, bf16[16,64,640]{2,1,0:T(8,128)(2,1)S(1)}, u32[]{:S(2)}) copy-start(bf16[16,64,640]{2,1,0:T(8,128)(2,1)S(1)} %copy.37) | copy-start | bytes 3932164
  125.5 10.1 %collective-permute-start = (bf16[1024,128]{1,0:T(8,128)(2,1)S(1)}, bf16[1024,128]{1,0:T(8,128)(2,1)S(1)}, u32[]{:S(2)}, u32[]{:S(2)}) collective-permute-start(bf16[1024,128]{1,0:T(8,128)(2,1)S(1)} %get-tuple-element.14), channel_id=1, source_target_pairs={{0,1},{1,2},{2,3},{3,4},{4,5},{5,6},{6,7},{7,8},{8,9},{9,10},{10,1... | collective-permute-start | bytes 786440 | tf_op jit(solution)/shard_map/ppermute | solution.py:18
  128.9 8.3 %collective-permute-start.1 = (bf16[1024,128]{1,0:T(8,128)(2,1)S(1)}, bf16[1024,128]{1,0:T(8,128)(2,1)S(1)}, u32[]{:S(2)}, u32[]{:S(2)}) collective-permute-start(bf16[1024,128]{1,0:T(8,128)(2,1)S(1)} %get-tuple-element.15), channel_id=1, source_target_pairs={{1,0},{2,1},{3,2},{4,3},{5,4},{6,5},{7,6},{8,7},{9,8},{10,9},{11,1... | collective-permute-start | bytes 786440 | tf_op jit(solution)/shard_map/ppermute | solution.py:21
  147.9 5.6 %copy-start.2 = (bf16[16,64,640]{2,1,0:T(8,128)(2,1)S(1)}, bf16[16,64,640]{2,1,0:T(8,128)(2,1)}, u32[]{:S(2)}) copy-start(bf16[16,64,640]{2,1,0:T(8,128)(2,1)} %copy-done.1) | copy-start | bytes 3932164
  155.2 1.2 copy-start.3
Sparse Core Ops, SparseCore 0:
  159.8 164.8 all-reduce.1
where the time goes:
time: 334 us; the launch traced here: 333 us
  waiting for transfers between devices  264 us (79%)
  local copies, waits for them, and re-layouts  20.4 us (6%)
  matrix products  15.7 us (5%)
  between operations  14.2 us (4%)
  starting transfers between devices  12.5 us (4%)
  other arithmetic  6.65 us (2%)
    psum x1, waiting for transfers between devices, per_device(): lax.psum(gram_part(moments, applied, 0, half_cols, total_rows), ('quad',...  164 us
    all_to_all x1, waiting for transfers between devices, per_device(): lax.all_to_all(solutions, 'quad', split_axis=3, concat_axis=0, tiled=True)  95.1 us
    unnamed x17, local copies, waits for them, and re-layouts  9.26 us
    all_to_all x1, starting transfers between devices, per_device(): lax.all_to_all(solutions, 'quad', split_axis=3, concat_axis=0, tiled=True)  7.53 us
  transfers between devices with their start and end apart: 4, of which 4 were waited for; matrix products, arithmetic and copies ran while one was open for 1% of the time, Pallas kernels for 0%

commit v1 on v0

v1 whole, which is shorter than its diff:
```python
import jax
import jax.numpy as jnp
from jax import lax
from jax.experimental import pallas as pl
from jax.experimental.pallas import tpu as pltpu
from jax.sharding import PartitionSpec as P

LCOL = 64
QPTS = 32
KMOM = 8
NB = 8
HALO = 2
LC = 16
BOTH = ("quad", "rows")
NT = (((1,), (1,)), ((), ()))


def moment_coefficients(angles, qweights):
    order = jnp.arange(KMOM, dtype=jnp.float32)[:, None]
    phase = order * angles[None, :]
    cosine = jnp.cos(phase)
    sine = jnp.sin(phase)
    real_coef = qweights[0][None, :] * cosine - qweights[1][None, :] * sine
    imag_coef = qweights[0][None, :] * sine + qweights[1][None, :] * cosine
    real_rows = jnp.stack([real_coef, -imag_coef], -1)
    imag_rows = jnp.stack([imag_coef, real_coef], -1)
    mixing = jnp.stack([real_rows, imag_rows], 0)
    return mixing.reshape(2 * KMOM, 2 * QPTS).astype(jnp.bfloat16)


def mixing_kernel(weights, received, moments):
    block = received[...]
    block = block.reshape(block.shape[0] * block.shape[1], block.shape[2])
    result = jnp.dot(weights[...], block, preferred_element_type=jnp.float32)
    moments[...] = result.astype(jnp.bfloat16).reshape(moments.shape)


def mix(wide, received):
    points, columns, rows = received.shape
    parts = 2 * KMOM
    return pl.pallas_call(
        mixing_kernel,
        grid=(columns // LC,),
        out_shape=jax.ShapeDtypeStruct((parts, columns, rows), jnp.bfloat16),
        in_specs=[
            pl.BlockSpec((parts * LC, points * LC), lambda i: (0, 0)),
            pl.BlockSpec((points, LC, rows), lambda i: (0, i, 0)),
        ],
        out_specs=pl.BlockSpec((parts, LC, rows), lambda i: (0, i, 0)),
        compiler_params=pltpu.CompilerParams(vmem_limit_bytes=32 * 2**20),
    )(wide, received)


def gram_kernel(low, moments, high, band, applied, gram):
    pairs, width, reach = band.shape
    rows = moments.shape[1]
    side = low.shape[1]
    half = moments.shape[0] // 2
    padded = jnp.concatenate([low[...], moments[...], high[...]], 1)
    for i in range(pairs):
        out = lax.dot_general(
            padded[:, i * width : i * width + reach], band[i], NT, preferred_element_type=jnp.float32
        )
        applied[:, i * width : (i + 1) * width] = out.astype(jnp.bfloat16)

    def prod(left, right):
        return lax.dot_general(left, right, NT, preferred_element_type=jnp.float32)

    real, imag = moments[:half, :], moments[half:, :]
    for m, right in enumerate((moments, applied)):
        other_real, other_imag = right[:half, :], right[half:, :]
        gram[:, (2 * m) * half : (2 * m + 1) * half] = prod(real, other_real) + prod(imag, other_imag)
        gram[:, (2 * m + 1) * half : (2 * m + 2) * half] = prod(real, other_imag) - prod(imag, other_real)


def apply_and_gram(low, moments, high, band):
    total, rows = moments.shape
    half = total // 2
    return pl.pallas_call(
        gram_kernel,
        out_shape=(
            jax.ShapeDtypeStruct((total, rows), jnp.bfloat16),
            jax.ShapeDtypeStruct((half, 4 * half), jnp.float32),
        ),
        in_specs=[pl.BlockSpec(memory_space=pltpu.VMEM)] * 4,
        out_specs=(pl.BlockSpec(memory_space=pltpu.VMEM),) * 2,
        compiler_params=pltpu.CompilerParams(vmem_limit_bytes=40 * 2**20),
    )(low, moments, high, band)


def band_blocks(neighbours, hblocks, first_cell):
    cells, orbitals, _ = hblocks.shape
    pairs = cells // 2
    window = 2 * HALO + 2
    local = (neighbours - first_cell + HALO).reshape(pairs, 2, NB) - 2 * jnp.arange(pairs)[:, None, None]
    split = hblocks.reshape(pairs, 2, orbitals, NB * orbitals)
    chosen = []
    for d in range(window):
        total = 0.0
        for n in range(NB):
            hit = (local[:, :, n] == d).astype(jnp.float32)[:, :, None, None]
            total += hit * split[:, :, :, n * orbitals : (n + 1) * orbitals].astype(jnp.float32)
        chosen.append(total.astype(jnp.bfloat16))
    return jnp.concatenate(chosen, -1).reshape(pairs, 2 * orbitals, window * orbitals)


def butterfly(gram, quads, rows):
    share = gram.shape[0] // quads
    me = lax.axis_index("quad")
    part = gram.reshape(quads, share, gram.shape[1])
    step = 1
    while step < quads:
        bit = (me // step) % 2
        split = part.reshape(part.shape[0] // 2, 2, share, part.shape[2])
        mine = lax.dynamic_index_in_dim(split, bit, 1, keepdims=False)
        other = lax.dynamic_index_in_dim(split, 1 - bit, 1, keepdims=False).astype(jnp.bfloat16)
        got = lax.ppermute(other, "quad", [(i, i ^ step) for i in range(quads)])
        part = mine + got.astype(jnp.float32)
        step *= 2
    part = part.reshape(share, gram.shape[1])
    step = 1
    while step < rows:
        part = part + lax.ppermute(part, "rows", [(i, i ^ step) for i in range(rows)])
        step *= 2
    return part


def per_device(solutions, angles, qweights, neighbours, hblocks):
    quads, rows = lax.axis_size("quad"), lax.axis_size("rows")
    groups = quads * rows
    rows_dev = solutions.shape[4]
    cells_dev = hblocks.shape[0]
    orbitals = hblocks.shape[1]
    half_cols = KMOM * LCOL
    mixing = moment_coefficients(angles, qweights)
    wide = (
        mixing[:, None, :, None] * jnp.eye(LC, dtype=jnp.bfloat16)[None, :, None, :]
    ).reshape(2 * KMOM * LC, 2 * QPTS * LC)
    first_cell = (lax.axis_index("quad") * rows + lax.axis_index("rows")) * cells_dev
    band = band_blocks(neighbours, hblocks, first_cell)
    received = lax.all_to_all(solutions, "quad", split_axis=3, concat_axis=0, tiled=True)
    stacked = received.reshape(QPTS * 2, LCOL, rows_dev)
    moments = mix(wide, stacked).reshape(2 * half_cols, rows_dev)
    side = HALO * orbitals
    forward = [(i, i + 1) for i in range(groups - 1)]
    backward = [(i + 1, i) for i in range(groups - 1)]
    low = lax.ppermute(moments[:, rows_dev - side :], BOTH, forward)
    high = lax.ppermute(moments[:, :side], BOTH, backward)
    applied, gram = apply_and_gram(low, moments, high, band)
    ritz = butterfly(gram, quads, rows) * (1.0 / (rows_dev * groups))
    return applied, ritz.reshape(half_cols // quads, 2, 2, half_cols)


def solution(mesh):
    in_specs = (
        P("quad", None, None, None, "rows"),
        P(),
        P(),
        P(BOTH, None),
        P(BOTH, None, None),
    )
    out_specs = (P(None, BOTH), P("quad", None, None, None))
    return jax.shard_map(
        per_device, mesh=mesh, in_specs=in_specs, out_specs=out_specs, check_vma=False
    )
```

time: 334 us -> 202 us (0.60)
  waiting for transfers between devices: 264 us -> 116 us
  starting transfers between devices: 12.5 us -> 43.5 us
  matrix products: 15.7 us -> 0 us
  between operations: 14.2 us -> 0.94 us
  Pallas kernels: 0 us -> 9.01 us
    psum x1 -> x0, waiting for transfers between devices: 164 us -> none  [per_device(): lax.psum(gram_part(moments, applied, 0, half_cols, total_rows), ('quad',...]
    ppermute x2 -> x7, waiting for transfers between devices: 5.32 us -> 36.8 us  [the longest x4 26.5 us: butterfly(): got = lax.ppermute(other, 'quad', [(i, i ^ step) for i in range(quads)])]
    ppermute x2 -> x7, starting transfers between devices: 4.91 us -> 36 us  [the longest x4 30.1 us: butterfly(): got = lax.ppermute(other, 'quad', [(i, i ^ step) for i in range(quads)])]
    all_to_all x1, waiting for transfers between devices: 95.1 us -> 79.1 us  [per_device(): lax.all_to_all(solutions, 'quad', split_axis=3, concat_axis=0, tiled=True)]
    dot_general x4 -> x0, matrix products: 15.7 us -> none  [the longest x1 6.5 us: per_device(): jnp.einsum('pq,qln->pln', mixing, stacked, preferred_element_type=jnp.flo...]
    pallas_call x0 -> x2, Pallas kernels: none -> 9.01 us  [the longest x1 4.57 us: mix(): pl.pallas_call(mixing_kernel, grid=(columns // LC,), out_shape=jax.ShapeD...]
    mul x0 -> x1, local copies, waits for them, and re-layouts: none -> 8.18 us  [per_device(): mixing[:, None, :, None] * jnp.eye(LC, dtype=jnp.bfloat16)[None, :, None, :]]
    gather x1 -> x0, local copies, waits for them, and re-layouts: 6.32 us -> none  [per_device(): jnp.take(cellwise, local_index, axis=1)]
  transfers between devices with their start and end apart: 4 -> 8, of which waited for: 4 -> 8; matrix products, arithmetic and copies ran while one was open for 1% -> 9% of each run, Pallas kernels for 0% -> 0%
where the time goes in v1:
time: 202 us; the launch traced here: 201 us
  waiting for transfers between devices  116 us (57%)
  starting transfers between devices  43.5 us (22%)
  local copies, waits for them, and re-layouts  23.6 us (12%)
  Pallas kernels  9.01 us (4%)
  other arithmetic  8.36 us (4%)
    all_to_all x1, waiting for transfers between devices, per_device(): lax.all_to_all(solutions, 'quad', split_axis=3, concat_axis=0, tiled=True)  79.1 us
    ppermute x4, starting transfers between devices, butterfly(): got = lax.ppermute(other, 'quad', [(i, i ^ step) for i in range(quads)])  30.1 us
    ppermute x4, waiting for transfers between devices, butterfly(): got = lax.ppermute(other, 'quad', [(i, i ^ step) for i in range(quads)])  26.5 us
    mul x1, local copies, waits for them, and re-layouts, per_device(): mixing[:, None, :, None] * jnp.eye(LC, dtype=jnp.bfloat16)[None, :, None, :]  8.18 us
    unnamed x11, local copies, waits for them, and re-layouts  8.05 us
    all_to_all x1, starting transfers between devices, per_device(): lax.all_to_all(solutions, 'quad', split_axis=3, concat_axis=0, tiled=True)  7.53 us
    ppermute x1, waiting for transfers between devices, butterfly(): lax.ppermute(part, 'rows', [(i, i ^ step) for i in range(rows)])  5.43 us
    pallas_call x1, Pallas kernels, mix(): pl.pallas_call(mixing_kernel, grid=(columns // LC,), out_shape=jax.ShapeD...  4.57 us
  transfers between devices with their start and end apart: 8, of which 8 were waited for; matrix products, arithmetic and copies ran while one was open for 9% of the time, Pallas kernels for 0%

profile of v1, /device:TPU:0, one launch (start us, length us, event | category | flops | bytes accessed | tf_op | source)
XLA Modules:
  0.0 201.3 jit_solution(13379848421148494013)
XLA Ops:
  0.6 6.1 %copy.409 = bf16[2,2,64,16,640]{4,2,1,0,3:T(8,128)(2,1)} copy(bf16[2,2,64,16,640]{4,3,2,1,0:T(8,128)(2,1)} %param.5) | data formatting | bytes 10485760 | tf_op args[0]
  6.7 7.5 %all-to-all-start = ((bf16[2,2,64,16,640]{4,2,1,0,3:T(8,128)(2,1)}), bf16[2,2,64,16,640]{4,2,1,0,3:T(8,128)(2,1)}, u32[]{:S(2)}, u32[]{:S(2)}) async-start(bf16[2,2,64,16,640]{4,2,1,0,3:T(8,128)(2,1)} %copy.409), calls=%async_computation | async-start | bytes 10485760 | tf_op jit(solution)/shard_map/all_to_all | solution.py:141
  14.7 2.4 %broadcast_multiply_fusion = bf16[16,16,64,16]{3,2,1,0:T(8,128)(2,1)} fusion(bf16[16,16]{1,0:T(8,128)(2,1)S(1)} %fusion.51, bf16[16,64]{1,0:T(8,128)(2,1)S(1)} %copy.408), kind=kLoop, calls=%fused_computation.2 | loop fusion | flops 262144 | bytes 526848 | tf_op jit(solution)/shard_map/mul | solution.py:137
  17.1 8.2 %mul.531.weights = bf16[256,1024]{1,0:T(8,128)(2,1)S(1)} reshape(bf16[16,16,64,16]{3,2,1,0:T(8,128)(2,1)} %broadcast_multiply_fusion) | data formatting | bytes 1048576 | tf_op jit(solution)/shard_map/mul | solution.py:137
  29.7 0.5 fusion.17
  30.2 0.5 fusion.25
  30.7 0.5 fusion.33
  31.1 79.1 %all-to-all-done = bf16[2,2,64,16,640]{4,2,1,0,3:T(8,128)(2,1)} async-done(((bf16[2,2,64,16,640]{4,2,1,0,3:T(8,128)(2,1)}), bf16[2,2,64,16,640]{4,2,1,0,3:T(8,128)(2,1)}, u32[]{:S(2)}, u32[]{:S(2)}) %all-to-all-start) | async-done | bytes 5242912 | tf_op jit(solution)/shard_map/all_to_all | solution.py:141
  110.2 4.6 %shard_map.68 = bf16[16,64,640]{2,1,0:T(8,128)(2,1)S(1)} custom-call(bf16[256,1024]{1,0:T(8,128)(2,1)S(1)} %mul.531.weights, bf16[64,64,640]{2,1,0:T(8,128)(2,1)} %bitcast.6.received), custom_call_target="tpu_custom_call" | custom-call | tf_op jit(solution)/shard_map/pallas_call | solution.py:41
  114.8 0.8 fusion.103
  115.6 3.4 %collective-permute-start = (bf16[1024,128]{1,0:T(8,128)(2,1)}, bf16[1024,128]{1,0:T(8,128)(2,1)S(1)}, u32[]{:S(2)}, u32[]{:S(2)}) collective-permute-start(bf16[1024,128]{1,0:T(8,128)(2,1)} %get-tuple-element.7), channel_id=1, source_target_pairs={{0,1},{1,2},{2,3},{3,4},{4,5},{5,6},{6,7},{7,8},{8,9},{9,10},{10,1... | collective-permute-start | bytes 786440 | tf_op jit(solution)/shard_map/ppermute | solution.py:147
  119.0 1.5 collective-permute-start.1
  120.5 0.5 fusion.41
  121.7 0.5 fusion.49
  122.2 0.5 concatenate.3
  122.7 3.3 %collective-permute-done.low = bf16[1024,128]{1,0:T(8,128)(2,1)S(1)} collective-permute-done((bf16[1024,128]{1,0:T(8,128)(2,1)}, bf16[1024,128]{1,0:T(8,128)(2,1)S(1)}, u32[]{:S(2)}, u32[]{:S(2)}) %collective-permute-start) | collective-permute-done | bytes 262176 | tf_op jit(solution)/shard_map/ppermute | solution.py:147
  126.0 1.5 collective-permute-done.1.high
  127.5 4.4 %shard_map.69 = (bf16[1024,640]{1,0:T(8,128)(2,1)}, f32[512,2048]{1,0:T(8,128)S(1)}) custom-call(bf16[1024,128]{1,0:T(8,128)(2,1)S(1)} %collective-permute-done.low, bf16[1024,640]{1,0:T(8,128)(2,1)S(1)} %bitcast.138, bf16[1024,128]{1,0:T(8,128)(2,1)S(1)} %collective-permute-done.1.high, bf16[5,128,384]{2,1,0:T(8,128)(2,1)S(1)} %bitcast.141), custom_call_target="tpu_custom_call" | custom-call | tf_op jit(solution)/shard_map/pallas_call | solution.py:79
  132.0 1.9 copy-done
  134.1 4.8 %collective-permute-start.2 = (bf16[8,32,2048]{2,1,0:T(8,128)(2,1)S(1)}, bf16[8,32,2048]{2,1,0:T(8,128)(2,1)S(1)}, u32[]{:S(2)}, u32[]{:S(2)}) collective-permute-start(bf16[8,32,2048]{2,1,0:T(8,128)(2,1)S(1)} %fusion), channel_id=1, source_target_pairs={{0,2},{2,0},{4,6},{6,4},{8,10},{10,8},{12,14},{14,12},{16,18},{18,... | collective-permute-start | bytes 3145736 | tf_op jit(solution)/shard_map/ppermute | solution.py:117
  138.9 2.3 %collective-permute-done.2 = bf16[8,32,2048]{2,1,0:T(8,128)(2,1)S(1)} collective-permute-done((bf16[8,32,2048]{2,1,0:T(8,128)(2,1)S(1)}, bf16[8,32,2048]{2,1,0:T(8,128)(2,1)S(1)}, u32[]{:S(2)}, u32[]{:S(2)}) %collective-permute-start.2) | collective-permute-done | bytes 1048608 | tf_op jit(solution)/shard_map/ppermute | solution.py:117
  141.2 1.8 bitcast_add_fusion
  143.1 13.2 %collective-permute-start.3 = (bf16[4,32,2048]{2,1,0:T(8,128)(2,1)S(1)}, bf16[4,32,2048]{2,1,0:T(8,128)(2,1)}, u32[]{:S(2)}, u32[]{:S(2)}) collective-permute-start(bf16[4,32,2048]{2,1,0:T(8,128)(2,1)S(1)} %fusion.1), channel_id=1, source_target_pairs={{0,4},{2,6},{4,0},{6,2},{8,12},{10,14},{12,8},{14,10},{16,20},{18,... | collective-permute-start | bytes 1572872 | tf_op jit(solution)/shard_map/ppermute | solution.py:117
  156.3 12.6 %collective-permute-done.3 = bf16[4,32,2048]{2,1,0:T(8,128)(2,1)} collective-permute-done((bf16[4,32,2048]{2,1,0:T(8,128)(2,1)S(1)}, bf16[4,32,2048]{2,1,0:T(8,128)(2,1)}, u32[]{:S(2)}, u32[]{:S(2)}) %collective-permute-start.3) | collective-permute-done | bytes 524320 | tf_op jit(solution)/shard_map/ppermute | solution.py:117
  168.8 1.1 bitcast_add_fusion.1
  170.0 9.4 %collective-permute-start.4 = (bf16[2,32,2048]{2,1,0:T(8,128)(2,1)S(1)}, bf16[2,32,2048]{2,1,0:T(8,128)(2,1)S(1)}, u32[]{:S(2)}, u32[]{:S(2)}) collective-permute-start(bf16[2,32,2048]{2,1,0:T(8,128)(2,1)S(1)} %fusion.50), channel_id=1, source_target_pairs={{0,8},{2,10},{4,12},{6,14},{8,0},{10,2},{12,4},{14,6},{16,24},{18,... | collective-permute-start | bytes 786440 | tf_op jit(solution)/shard_map/ppermute | solution.py:117
  179.4 6.1 %collective-permute-done.4 = bf16[2,32,2048]{2,1,0:T(8,128)(2,1)S(1)} collective-permute-done((bf16[2,32,2048]{2,1,0:T(8,128)(2,1)S(1)}, bf16[2,32,2048]{2,1,0:T(8,128)(2,1)S(1)}, u32[]{:S(2)}, u32[]{:S(2)}) %collective-permute-start.4) | collective-permute-done | bytes 262176 | tf_op jit(solution)/shard_map/ppermute | solution.py:117
  185.6 2.7 %collective-permute-start.5 = (bf16[1,32,2048]{2,1,0:T(8,128)(2,1)S(1)}, bf16[1,32,2048]{2,1,0:T(8,128)(2,1)S(1)}, u32[]{:S(2)}, u32[]{:S(2)}) collective-permute-start(bf16[1,32,2048]{2,1,0:T(8,128)(2,1)S(1)} %dynamic-slice_convert_fusion.2), channel_id=1, source_target_pairs={{0,16},{2,18},{4,20},{6,22},{8,24},{10,26},{12,28},{14,30},{16,0},... | collective-permute-start | bytes 393224 | tf_op jit(solution)/shard_map/ppermute | solution.py:117
  188.3 5.6 %collective-permute-done.5 = bf16[1,32,2048]{2,1,0:T(8,128)(2,1)S(1)} collective-permute-done((bf16[1,32,2048]{2,1,0:T(8,128)(2,1)S(1)}, bf16[1,32,2048]{2,1,0:T(8,128)(2,1)S(1)}, u32[]{:S(2)}, u32[]{:S(2)}) %collective-permute-start.5) | collective-permute-done | bytes 131104 | tf_op jit(solution)/shard_map/ppermute | solution.py:117
  193.9 1.0 collective-permute-start.6
  194.9 5.4 %collective-permute-done.6 = f32[32,2048]{1,0:T(8,128)S(1)} collective-permute-done((f32[32,2048]{1,0:T(8,128)S(1)}, f32[32,2048]{1,0:T(8,128)S(1)}, u32[]{:S(2)}, u32[]{:S(2)}) %collective-permute-start.6) | collective-permute-done | bytes 262176 | tf_op jit(solution)/shard_map/ppermute | solution.py:123
  200.3 0.9 reshape.817
  (82 shorter events, 5.9 us)
Async XLA Ops:
  6.7 7.6 %copy-start.3 = (f32[2,32]{1,0:T(2,128)S(1)}, f32[2,32]{1,0:T(2,128)}, u32[]{:S(2)}) copy-start(f32[2,32]{1,0:T(2,128)} %param.7) | copy-start | bytes 772
  6.7 7.6 %copy-start.4 = (f32[32]{0:T(128)S(1)}, f32[32]{0:T(128)}, u32[]{:S(2)}) copy-start(f32[32]{0:T(128)} %param.6) | copy-start | bytes 388
  6.7 103.5 %all-to-all-start = ((bf16[2,2,64,16,640]{4,2,1,0,3:T(8,128)(2,1)}), bf16[2,2,64,16,640]{4,2,1,0,3:T(8,128)(2,1)}, u32[]{:S(2)}, u32[]{:S(2)}) async-start(bf16[2,2,64,16,640]{4,2,1,0,3:T(8,128)(2,1)} %copy.409), calls=%async_computation | async-start | bytes 10485760 | tf_op jit(solution)/shard_map/all_to_all | solution.py:141
  14.7 10.6 %copy-start.2 = (s32[10,8]{0,1:T(8,128)S(1)}, s32[10,8]{0,1:T(8,128)}, u32[]{:S(2)}) copy-start(s32[10,8]{0,1:T(8,128)} %param.8) | copy-start | bytes 964
  14.7 14.6 %copy-start.1 = (bf16[10,64,512]{2,1,0:T(8,128)(2,1)S(1)}, bf16[10,64,512]{2,1,0:T(8,128)(2,1)}, u32[]{:S(2)}) copy-start(bf16[10,64,512]{2,1,0:T(8,128)(2,1)} %param.9) | copy-start | bytes 1966084
  115.6 10.4 %collective-permute-start = (bf16[1024,128]{1,0:T(8,128)(2,1)}, bf16[1024,128]{1,0:T(8,128)(2,1)S(1)}, u32[]{:S(2)}, u32[]{:S(2)}) collective-permute-start(bf16[1024,128]{1,0:T(8,128)(2,1)} %get-tuple-element.7), channel_id=1, source_target_pairs={{0,1},{1,2},{2,3},{3,4},{4,5},{5,6},{6,7},{7,8},{8,9},{9,10},{10,1... | collective-permute-start | bytes 786440 | tf_op jit(solution)/shard_map/ppermute | solution.py:147
  119.0 8.5 %collective-permute-start.1 = (bf16[1024,128]{1,0:T(8,128)(2,1)}, bf16[1024,128]{1,0:T(8,128)(2,1)S(1)}, u32[]{:S(2)}, u32[]{:S(2)}) collective-permute-start(bf16[1024,128]{1,0:T(8,128)(2,1)} %get-tuple-element.6), channel_id=1, source_target_pairs={{1,0},{2,1},{3,2},{4,3},{5,4},{6,5},{7,6},{8,7},{9,8},{10,9},{11,1... | collective-permute-start | bytes 786440 | tf_op jit(solution)/shard_map/ppermute | solution.py:148
  132.0 1.9 copy-start
  134.1 7.1 %collective-permute-start.2 = (bf16[8,32,2048]{2,1,0:T(8,128)(2,1)S(1)}, bf16[8,32,2048]{2,1,0:T(8,128)(2,1)S(1)}, u32[]{:S(2)}, u32[]{:S(2)}) collective-permute-start(bf16[8,32,2048]{2,1,0:T(8,128)(2,1)S(1)} %fusion), channel_id=1, source_target_pairs={{0,2},{2,0},{4,6},{6,4},{8,10},{10,8},{12,14},{14,12},{16,18},{18,... | collective-permute-start | bytes 3145736 | tf_op jit(solution)/shard_map/ppermute | solution.py:117
  143.1 25.8 %collective-permute-start.3 = (bf16[4,32,2048]{2,1,0:T(8,128)(2,1)S(1)}, bf16[4,32,2048]{2,1,0:T(8,128)(2,1)}, u32[]{:S(2)}, u32[]{:S(2)}) collective-permute-start(bf16[4,32,2048]{2,1,0:T(8,128)(2,1)S(1)} %fusion.1), channel_id=1, source_target_pairs={{0,4},{2,6},{4,0},{6,2},{8,12},{10,14},{12,8},{14,10},{16,20},{18,... | collective-permute-start | bytes 1572872 | tf_op jit(solution)/shard_map/ppermute | solution.py:117
  170.0 15.5 %collective-permute-start.4 = (bf16[2,32,2048]{2,1,0:T(8,128)(2,1)S(1)}, bf16[2,32,2048]{2,1,0:T(8,128)(2,1)S(1)}, u32[]{:S(2)}, u32[]{:S(2)}) collective-permute-start(bf16[2,32,2048]{2,1,0:T(8,128)(2,1)S(1)} %fusion.50), channel_id=1, source_target_pairs={{0,8},{2,10},{4,12},{6,14},{8,0},{10,2},{12,4},{14,6},{16,24},{18,... | collective-permute-start | bytes 786440 | tf_op jit(solution)/shard_map/ppermute | solution.py:117
  185.6 8.2 %collective-permute-start.5 = (bf16[1,32,2048]{2,1,0:T(8,128)(2,1)S(1)}, bf16[1,32,2048]{2,1,0:T(8,128)(2,1)S(1)}, u32[]{:S(2)}, u32[]{:S(2)}) collective-permute-start(bf16[1,32,2048]{2,1,0:T(8,128)(2,1)S(1)} %dynamic-slice_convert_fusion.2), channel_id=1, source_target_pairs={{0,16},{2,18},{4,20},{6,22},{8,24},{10,26},{12,28},{14,30},{16,0},... | collective-permute-start | bytes 393224 | tf_op jit(solution)/shard_map/ppermute | solution.py:117
  193.9 6.4 %collective-permute-start.6 = (f32[32,2048]{1,0:T(8,128)S(1)}, f32[32,2048]{1,0:T(8,128)S(1)}, u32[]{:S(2)}, u32[]{:S(2)}) collective-permute-start(f32[32,2048]{1,0:T(8,128)S(1)} %add_bitcast_fusion), channel_id=1, source_target_pairs={{0,1},{1,0},{2,3},{3,2},{4,5},{5,4},{6,7},{7,6},{8,9},{9,8},{10,11... | collective-permute-start | bytes 786440 | tf_op jit(solution)/shard_map/ppermute | solution.py:123

commit v2 on v1

v2 whole, which is shorter than its diff:
```python
import functools

import jax
import jax.numpy as jnp
from jax import lax
from jax.experimental import pallas as pl
from jax.experimental.pallas import tpu as pltpu
from jax.sharding import PartitionSpec as P

LCOL = 64
QPTS = 32
KMOM = 8
NB = 8
HALO = 2
LC = 16
BOTH = ("quad", "rows")
NT = (((1,), (1,)), ((), ()))
MESH = pl.DeviceIdType.MESH


def moment_coefficients(angles, qweights):
    order = jnp.arange(KMOM, dtype=jnp.float32)[:, None]
    phase = order * angles[None, :]
    cosine = jnp.cos(phase)
    sine = jnp.sin(phase)
    real_coef = qweights[0][None, :] * cosine - qweights[1][None, :] * sine
    imag_coef = qweights[0][None, :] * sine + qweights[1][None, :] * cosine
    real_rows = jnp.stack([real_coef, -imag_coef], -1)
    imag_rows = jnp.stack([imag_coef, real_coef], -1)
    mixing = jnp.stack([real_rows, imag_rows], 0)
    return mixing.reshape(2 * KMOM, 2 * QPTS).astype(jnp.bfloat16)


def step_plan(quads):
    bits = quads.bit_length() - 1
    rising = [(1 << i, True) for i in range(bits)]
    falling = [(1, True)] + [(1 << i, False) for i in range(bits - 1, 0, -1)]
    return rising, falling


def fused_kernel(
    quads, groups_r, scale, solutions, mixing, band, applied, ritz,
    outgoing, incoming, moments, low, high, wide, gram, sent, got, last, last_got,
    own_sem, a2a_send, a2a_recv, halo_send, halo_recv, step_send, step_recv, row_send, row_recv,
):
    points, columns, owners, rows = solutions.shape
    chunks = columns // LC
    parts = 2 * KMOM
    half = KMOM * columns
    share = half // quads
    pairs, width, reach = band.shape
    side = low.shape[-1]
    me = lax.axis_index("quad")
    row = lax.axis_index("rows")
    flat = me * groups_r + row
    total = quads * groups_r
    after, before = lax.rem(flat + 1, total), lax.rem(flat + total - 1, total)
    after = {"quad": after // groups_r, "rows": lax.rem(after, groups_r)}
    before = {"quad": before // groups_r, "rows": lax.rem(before, groups_r)}
    row_steps = [1 << i for i in range(groups_r.bit_length() - 1)]

    def partner(index, step):
        return index + step - 2 * step * lax.rem(index // step, 2)

    def copy_out(c, o):
        target = lax.rem(me + o, quads)
        return pltpu.make_async_remote_copy(
            src_ref=outgoing.at[c, target],
            dst_ref=incoming.at[c, pl.ds(me * points, points)],
            send_sem=a2a_send.at[c, o],
            recv_sem=a2a_recv.at[c, o],
            device_id={"quad": target},
            device_id_type=MESH,
        )

    def own_copy(c):
        return pltpu.make_async_copy(
            outgoing.at[c, me], incoming.at[c, pl.ds(me * points, points)], own_sem.at[c]
        )

    size = owners * LC
    r_index = lax.broadcasted_iota(jnp.int32, (size, size), 0)
    c_index = lax.broadcasted_iota(jnp.int32, (size, size), 1)
    swap = jnp.where(
        (r_index // LC == lax.rem(c_index, owners)) & (lax.rem(r_index, LC) == c_index // owners), 1.0, 0.0
    ).astype(jnp.bfloat16)

    def rearrange(c):
        def one(q, carry):
            block = solutions[q, c * LC : (c + 1) * LC].reshape(size, rows)
            moved = jnp.dot(swap, block, preferred_element_type=jnp.float32).astype(jnp.bfloat16)
            outgoing[c, :, q] = moved.reshape(owners, LC, rows)
            return carry

        lax.fori_loop(0, points, one, 0)

    barrier = pltpu.get_barrier_semaphore()

    def greet(o, carry):
        pl.semaphore_signal(
            barrier, inc=1, device_id={"quad": lax.rem(me + o, quads)}, device_id_type=MESH
        )
        return carry

    lax.fori_loop(1, quads, greet, 0)
    pl.semaphore_signal(barrier, inc=1, device_id=after, device_id_type=MESH)
    pl.semaphore_signal(barrier, inc=1, device_id=before, device_id_type=MESH)
    for step in row_steps:
        pl.semaphore_signal(
            barrier, inc=1, device_id={"rows": partner(row, step)}, device_id_type=MESH
        )
    rearrange(0)
    pl.semaphore_wait(barrier, quads + 1 + len(row_steps))

    for c in range(chunks):
        if c:
            rearrange(c)

        def send(o, carry):
            copy_out(c, o).start()
            return carry

        lax.fori_loop(1, quads, send, 0)
        own_copy(c).start()

    high_rows, deep = wide.shape
    spread_p = jnp.where(
        lax.broadcasted_iota(jnp.int32, (high_rows, parts), 0) // LC
        == lax.broadcasted_iota(jnp.int32, (high_rows, parts), 1), 1.0, 0.0,
    ).astype(jnp.bfloat16)
    spread_q = jnp.where(
        lax.broadcasted_iota(jnp.int32, (deep // LC, deep), 1) // LC
        == lax.broadcasted_iota(jnp.int32, (deep // LC, deep), 0), 1.0, 0.0,
    ).astype(jnp.bfloat16)
    tall = jnp.dot(spread_p, mixing[...], preferred_element_type=jnp.float32).astype(jnp.bfloat16)
    full = jnp.dot(tall, spread_q, preferred_element_type=jnp.float32)
    same = lax.rem(lax.broadcasted_iota(jnp.int32, (high_rows, deep), 0), LC) == lax.rem(
        lax.broadcasted_iota(jnp.int32, (high_rows, deep), 1), LC
    )
    wide[...] = jnp.where(same, full, 0.0).astype(jnp.bfloat16)

    def halo_copies(c):
        up = pltpu.make_async_remote_copy(
            src_ref=moments.at[:, c, :, rows - side : rows],
            dst_ref=low.at[:, c],
            send_sem=halo_send.at[0, c],
            recv_sem=halo_recv.at[0, c],
            device_id=after,
            device_id_type=MESH,
        )
        down = pltpu.make_async_remote_copy(
            src_ref=moments.at[:, c, :, 0:side],
            dst_ref=high.at[:, c],
            send_sem=halo_send.at[1, c],
            recv_sem=halo_recv.at[1, c],
            device_id=before,
            device_id_type=MESH,
        )
        return up, down

    def apply_band(c):
        for copy in halo_copies(c):
            copy.wait_recv()
        near = jnp.concatenate([low[:, c], moments[:, c], high[:, c]], -1)
        near = near.reshape(parts * LC, rows + 2 * side)
        for i in range(pairs):
            out = lax.dot_general(
                near[:, i * width : i * width + reach], band[i], NT, preferred_element_type=jnp.float32
            )
            applied[:, c, :, i * width : (i + 1) * width] = out.astype(jnp.bfloat16).reshape(
                parts, LC, width
            )

    for c in range(chunks):
        own_copy(c).wait()

        def arrive(o, carry):
            copy_out(c, o).wait_recv()
            return carry

        lax.fori_loop(1, quads, arrive, 0)
        block = incoming[c].reshape(deep, rows)
        mixed = jnp.dot(wide[...], block, preferred_element_type=jnp.float32)
        moments[:, c] = mixed.astype(jnp.bfloat16).reshape(parts, LC, rows)
        for copy in halo_copies(c):
            copy.start()
        if c:
            apply_band(c - 1)

    def prod(left, right):
        return lax.dot_general(left, right, NT, preferred_element_type=jnp.float32)

    def grams(m, right):
        real = moments[:KMOM].reshape(half, rows)
        imag = moments[KMOM:].reshape(half, rows)
        other_real = right[:KMOM].reshape(half, rows)
        other_imag = right[KMOM:].reshape(half, rows)
        plain = prod(real, other_real) + prod(imag, other_imag)
        gram[m, :, :, :half] = plain.reshape(quads, share, half)
        cross = prod(real, other_imag) - prod(imag, other_real)
        gram[m, :, :, half:] = cross.reshape(quads, share, half)

    plans = step_plan(quads)
    steps = len(plans[0])

    def place(s):
        return quads - (quads >> s)

    def step_copy(m, s):
        bit, _ = plans[m][s]
        count = quads >> (s + 1)
        return pltpu.make_async_remote_copy(
            src_ref=sent.at[m, pl.ds(place(s), count)],
            dst_ref=got.at[m, pl.ds(place(s), count)],
            send_sem=step_send.at[m, s],
            recv_sem=step_recv.at[m, s],
            device_id={"quad": partner(me, bit)},
            device_id_type=MESH,
        )

    def position(m, s, j, side_bit):
        _, rising = plans[m][s]
        count = quads >> (s + 1)
        return 2 * j + side_bit if rising else j + side_bit * count

    def pack(m, s):
        bit, _ = plans[m][s]
        mine = lax.rem(me // bit, 2)

        def one(j, carry):
            sent[m, place(s) + j] = gram[m, position(m, s, j, 1 - mine)].astype(jnp.bfloat16)
            return carry

        lax.fori_loop(0, quads >> (s + 1), one, 0)
        step_copy(m, s).start()

    def gather(m, s):
        bit, _ = plans[m][s]
        mine = lax.rem(me // bit, 2)
        step_copy(m, s).wait_recv()

        def one(j, carry):
            gram[m, j] = gram[m, position(m, s, j, mine)] + got[m, place(s) + j].astype(jnp.float32)
            return carry

        lax.fori_loop(0, quads >> (s + 1), one, 0)

    def row_copy(m, s):
        return pltpu.make_async_remote_copy(
            src_ref=last.at[m, s],
            dst_ref=last_got.at[m, s],
            send_sem=row_send.at[m, s],
            recv_sem=row_recv.at[m, s],
            device_id={"rows": partner(row, row_steps[s])},
            device_id_type=MESH,
        )

    grams(0, moments)
    pack(0, 0)
    apply_band(chunks - 1)
    grams(1, applied)
    pack(1, 0)
    for s in range(steps):
        for m in range(2):
            gather(m, s)
            if s + 1 < steps:
                pack(m, s + 1)
            else:
                last[m, 0] = gram[m, 0]
                row_copy(m, 0).start()
    for s in range(len(row_steps)):
        for m in range(2):
            row_copy(m, s).wait_recv()
            summed = last[m, s] + last_got[m, s]
            if s + 1 < len(row_steps):
                last[m, s + 1] = summed
                row_copy(m, s + 1).start()
            else:
                ritz[:, 2 * m * half : 2 * (m + 1) * half] = summed * scale

    for c in range(chunks):

        def leave(o, carry):
            copy_out(c, o).wait_send()
            return carry

        lax.fori_loop(1, quads, leave, 0)
        for copy in halo_copies(c):
            copy.wait_send()
    for m in range(2):
        for s in range(steps):
            step_copy(m, s).wait_send()
        for s in range(len(row_steps)):
            row_copy(m, s).wait_send()


def fused(solutions, mixing, band, quads, groups_r, scale):
    points, columns, owners, rows = solutions.shape
    chunks = columns // LC
    parts = 2 * KMOM
    half = KMOM * columns
    share = half // quads
    side = (band.shape[2] - band.shape[1]) // 2
    steps = quads.bit_length() - 1
    row_steps = groups_r.bit_length() - 1
    bf, f4 = jnp.bfloat16, jnp.float32
    dma = pltpu.SemaphoreType.DMA
    return pl.pallas_call(
        functools.partial(fused_kernel, quads, groups_r, scale),
        out_shape=(
            jax.ShapeDtypeStruct((parts, chunks, LC, rows), bf),
            jax.ShapeDtypeStruct((share, 4 * half), f4),
        ),
        in_specs=[pl.BlockSpec(memory_space=pltpu.VMEM)] * 3,
        out_specs=(pl.BlockSpec(memory_space=pltpu.VMEM),) * 2,
        scratch_shapes=[
            pltpu.VMEM((chunks, owners, points, LC, rows), bf),
            pltpu.VMEM((chunks, owners * points, LC, rows), bf),
            pltpu.VMEM((parts, chunks, LC, rows), bf),
            pltpu.VMEM((parts, chunks, LC, side), bf),
            pltpu.VMEM((parts, chunks, LC, side), bf),
            pltpu.VMEM((parts * LC, owners * points * LC), bf),
            pltpu.VMEM((2, quads, share, 2 * half), f4),
            pltpu.VMEM((2, quads, share, 2 * half), bf),
            pltpu.VMEM((2, quads, share, 2 * half), bf),
            pltpu.VMEM((2, row_steps, share, 2 * half), f4),
            pltpu.VMEM((2, row_steps, share, 2 * half), f4),
            dma((chunks,)),
            dma((chunks, quads)),
            dma((chunks, quads)),
            dma((2, chunks)),
            dma((2, chunks)),
            dma((2, steps)),
            dma((2, steps)),
            dma((2, row_steps)),
            dma((2, row_steps)),
        ],
        compiler_params=pltpu.CompilerParams(
            collective_id=0, has_side_effects=True, vmem_limit_bytes=56 * 2**20
        ),
    )(solutions, mixing, band)


def band_blocks(neighbours, hblocks, first_cell):
    cells, orbitals, _ = hblocks.shape
    pairs = cells // 2
    window = 2 * HALO + 2
    local = (neighbours - first_cell + HALO).reshape(pairs, 2, NB) - 2 * jnp.arange(pairs)[:, None, None]
    split = hblocks.reshape(pairs, 2, orbitals, NB * orbitals)
    chosen = []
    for d in range(window):
        total = 0.0
        for n in range(NB):
            hit = (local[:, :, n] == d).astype(jnp.float32)[:, :, None, None]
            total += hit * split[:, :, :, n * orbitals : (n + 1) * orbitals].astype(jnp.float32)
        chosen.append(total.astype(jnp.bfloat16))
    return jnp.concatenate(chosen, -1).reshape(pairs, 2 * orbitals, window * orbitals)


def per_device(solutions, angles, qweights, neighbours, hblocks):
    quads, rows = lax.axis_size("quad"), lax.axis_size("rows")
    rows_dev = solutions.shape[4]
    cells_dev = hblocks.shape[0]
    half_cols = KMOM * LCOL
    mixing = moment_coefficients(angles, qweights)
    first_cell = (lax.axis_index("quad") * rows + lax.axis_index("rows")) * cells_dev
    band = band_blocks(neighbours, hblocks, first_cell)
    shaped = solutions.reshape((-1,) + solutions.shape[2:])
    applied, ritz = fused(shaped, mixing, band, quads, rows, 1.0 / (rows_dev * quads * rows))
    return (
        applied.reshape(2 * half_cols, rows_dev),
        ritz.reshape(half_cols // quads, 2, 2, half_cols),
    )


def solution(mesh):
    in_specs = (
        P("quad", None, None, None, "rows"),
        P(),
        P(),
        P(BOTH, None),
        P(BOTH, None, None),
    )
    out_specs = (P(None, BOTH), P("quad", None, None, None))
    return jax.shard_map(
        per_device, mesh=mesh, in_specs=in_specs, out_specs=out_specs, check_vma=False
    )
```

time: 202 us -> 180 us (0.89)
  Pallas kernels: 9.01 us -> 163 us
  waiting for transfers between devices: 116 us -> 0 us
  starting transfers between devices: 43.5 us -> 0 us
  local copies, waits for them, and re-layouts: 23.6 us -> 11.7 us
  other arithmetic: 8.36 us -> 4.18 us
    pallas_call x2 -> x1, Pallas kernels: 9.01 us -> 163 us  [fused(): pl.pallas_call(functools.partial(fused_kernel, quads, groups_r, scale), o...]
    all_to_all x1 -> x0, waiting for transfers between devices: 79.1 us -> none  [per_device(): lax.all_to_all(solutions, 'quad', split_axis=3, concat_axis=0, tiled=True)]
    ppermute x7 -> x0, waiting for transfers between devices: 36.8 us -> none  [the longest x4 26.5 us: butterfly(): got = lax.ppermute(other, 'quad', [(i, i ^ step) for i in range(quads)])]
    ppermute x7 -> x0, starting transfers between devices: 36 us -> none  [the longest x4 30.1 us: butterfly(): got = lax.ppermute(other, 'quad', [(i, i ^ step) for i in range(quads)])]
    mul x1 -> x0, local copies, waits for them, and re-layouts: 8.18 us -> none  [per_device(): mixing[:, None, :, None] * jnp.eye(LC, dtype=jnp.bfloat16)[None, :, None, :]]
    all_to_all x1 -> x0, starting transfers between devices: 7.53 us -> none  [per_device(): lax.all_to_all(solutions, 'quad', split_axis=3, concat_axis=0, tiled=True)]
    unnamed x11 -> x3, local copies, waits for them, and re-layouts: 8.05 us -> 2.49 us
    add x3 -> x0, other arithmetic: 3.03 us -> none  [butterfly(): part = mine + got.astype(jnp.float32)]
  transfers between devices with their start and end apart: 8 -> 0, of which waited for: 8 -> 0; matrix products, arithmetic and copies ran while one was open for 9% -> 0% of each run, Pallas kernels for 0% -> 0%
where the time goes in v2:
time: 180 us
  Pallas kernels  163 us (91%)
  local copies, waits for them, and re-layouts  11.7 us (6%)
  other arithmetic  4.18 us (2%)
    pallas_call x1, Pallas kernels, fused(): pl.pallas_call(functools.partial(fused_kernel, quads, groups_r, scale), o...  163 us
    convert_element_type x48, local copies, waits for them, and re-layouts, band_blocks(): hit = (local[:, :, n] == d).astype(jnp.float32)[:, :, None, None]  4.42 us

profile of v2, /device:TPU:0, one launch (start us, length us, event | category | flops | bytes accessed | tf_op | source)
XLA Modules:
  0.0 180.2 jit_solution(16299142891720563166)
XLA Ops:
  0.7 0.8 slice_bitcast_fusion.1
  1.4 0.7 subtract_add_fusion
  2.2 0.1 copy.304
  2.3 0.7 negate_convert_fusion
  3.1 0.1 copy.352
  3.2 0.1 copy.344
  3.3 0.1 copy.312
  3.3 0.1 copy.311
  3.4 0.1 copy.310
  3.9 0.1 copy.305
  4.4 0.1 copy.341
  4.6 0.1 copy.318
  5.0 0.1 copy.319
  5.5 0.1 copy.320
  5.7 0.1 copy.336
  6.1 0.1 copy.337
  6.6 0.1 copy.346
  6.8 0.1 copy.323
  7.3 0.1 copy.324
  7.4 0.1 copy.340
  7.5 0.1 copy.302
  7.7 0.7 copy.353.mixing
  8.4 0.5 fusion.39
  8.9 0.5 fusion.31
  9.3 0.5 fusion.23
  9.8 0.5 fusion.15
  10.3 0.5 fusion.47
  10.7 0.5 fusion.7
  11.2 1.1 concatenate.3
  12.3 163.5 %shard_map.68 = (bf16[16,4,16,640]{3,2,1,0:T(8,128)(2,1)}, f32[32,2048]{1,0:T(8,128)}) custom-call(bf16[4,64,16,640]{3,2,1,0:T(8,128)(2,1)} %bitcast.116, bf16[16,64]{1,0:T(8,128)(2,1)} %copy.353.mixing, bf16[5,128,384]{2,1,0:T(8,128)(2,1)} %bitcast.117), custom_call_target="tpu_custom_call" | custom-call | tf_op jit(solution)/shard_map/pallas_call | solution.py:308
  175.8 1.9 %reshape.777 = f32[32,2,2,512]{3,2,1,0:T(2,128)} reshape(f32[32,2048]{1,0:T(8,128)} %get-tuple-element.5) | data formatting | bytes 524288 | tf_op jit(solution)/shard_map/reshape | solution.py:372
  177.7 2.5 %copy.355 = bf16[1024,640]{1,0:T(8,128)(2,1)} copy(bf16[1024,640]{1,0:T(8,128)(2,1)} %bitcast.118) | data formatting | bytes 2621440
  (44 shorter events, 3.2 us)
Async XLA Ops:
  0.6 7.8 %copy-start = (bf16[10,64,512]{2,1,0:T(8,128)(2,1)S(1)}, bf16[10,64,512]{2,1,0:T(8,128)(2,1)}, u32[]{:S(2)}) copy-start(bf16[10,64,512]{2,1,0:T(8,128)(2,1)} %param.9) | copy-start | bytes 1966084

commit v3 on v2

--- a/solution.py
+++ b/solution.py
@@ -13,6 +13,7 @@
 NB = 8
 HALO = 2
 LC = 16
+LINE = 4
 BOTH = ("quad", "rows")
 NT = (((1,), (1,)), ((), ()))
 MESH = pl.DeviceIdType.MESH
@@ -40,8 +41,8 @@
 
 def fused_kernel(
     quads, groups_r, scale, solutions, mixing, band, applied, ritz,
-    outgoing, incoming, moments, low, high, wide, gram, sent, got, last, last_got,
-    own_sem, a2a_send, a2a_recv, halo_send, halo_recv, step_send, step_recv, row_send, row_recv,
+    outgoing, incoming, passed, landed, moments, low, high, wide, gram, sent, got, last, last_got,
+    own_sem, a2a_send, a2a_recv, line_send, line_recv, halo_send, halo_recv, step_send, step_recv, row_send, row_recv,
 ):
     points, columns, owners, rows = solutions.shape
     chunks = columns // LC
@@ -62,47 +63,57 @@
     def partner(index, step):
         return index + step - 2 * step * lax.rem(index // step, 2)
 
+    group = quads // LINE
+    spot = lax.rem(me, group)
+    line = me // group
+
     def copy_out(c, o):
-        target = lax.rem(me + o, quads)
+        target = lax.rem(spot + o, group)
         return pltpu.make_async_remote_copy(
             src_ref=outgoing.at[c, target],
-            dst_ref=incoming.at[c, pl.ds(me * points, points)],
+            dst_ref=incoming.at[c, spot],
             send_sem=a2a_send.at[c, o],
             recv_sem=a2a_recv.at[c, o],
-            device_id={"quad": target},
+            device_id={"quad": line * group + target},
             device_id_type=MESH,
         )
 
     def own_copy(c):
-        return pltpu.make_async_copy(
-            outgoing.at[c, me], incoming.at[c, pl.ds(me * points, points)], own_sem.at[c]
+        return pltpu.make_async_copy(outgoing.at[c, spot], incoming.at[c, spot], own_sem.at[c])
+
+    def line_copy(c, slot, landing, shift):
+        return pltpu.make_async_remote_copy(
+            src_ref=passed.at[c, slot],
+            dst_ref=landed.at[c, landing],
+            send_sem=line_send.at[c, slot],
+            recv_sem=line_recv.at[c, landing],
+            device_id={"quad": lax.rem(me + shift + quads, quads)},
+            device_id_type=MESH,
         )
 
     size = owners * LC
     r_index = lax.broadcasted_iota(jnp.int32, (size, size), 0)
     c_index = lax.broadcasted_iota(jnp.int32, (size, size), 1)
     swap = jnp.where(
-        (r_index // LC == lax.rem(c_index, owners)) & (lax.rem(r_index, LC) == c_index // owners), 1.0, 0.0
+        (lax.rem(r_index // LC, LINE) * group + r_index // (LC * LINE) == lax.rem(c_index, owners)) & (lax.rem(r_index, LC) == c_index // owners), 1.0, 0.0
     ).astype(jnp.bfloat16)
 
     def rearrange(c):
         def one(q, carry):
             block = solutions[q, c * LC : (c + 1) * LC].reshape(size, rows)
             moved = jnp.dot(swap, block, preferred_element_type=jnp.float32).astype(jnp.bfloat16)
-            outgoing[c, :, q] = moved.reshape(owners, LC, rows)
+            outgoing[c, :, :, q] = moved.reshape(group, LINE, LC, rows)
             return carry
 
         lax.fori_loop(0, points, one, 0)
 
     barrier = pltpu.get_barrier_semaphore()
 
-    def greet(o, carry):
-        pl.semaphore_signal(
-            barrier, inc=1, device_id={"quad": lax.rem(me + o, quads)}, device_id_type=MESH
-        )
-        return carry
-
-    lax.fori_loop(1, quads, greet, 0)
+    near_by = [line * group + lax.rem(spot + o, group) for o in range(1, group)]
+    near_by += [lax.rem(me + group, quads), lax.rem(me + quads - group, quads)]
+    near_by += [partner(me, 1 << b) for b in range(quads.bit_length() - 1)]
+    for other in near_by:
+        pl.semaphore_signal(barrier, inc=1, device_id={"quad": other}, device_id_type=MESH)
     pl.semaphore_signal(barrier, inc=1, device_id=after, device_id_type=MESH)
     pl.semaphore_signal(barrier, inc=1, device_id=before, device_id_type=MESH)
     for step in row_steps:
@@ -110,7 +121,7 @@
             barrier, inc=1, device_id={"rows": partner(row, step)}, device_id_type=MESH
         )
     rearrange(0)
-    pl.semaphore_wait(barrier, quads + 1 + len(row_steps))
+    pl.semaphore_wait(barrier, len(near_by) + 2 + len(row_steps))
 
     for c in range(chunks):
         if c:
@@ -120,7 +131,7 @@
             copy_out(c, o).start()
             return carry
 
-        lax.fori_loop(1, quads, send, 0)
+        lax.fori_loop(1, group, send, 0)
         own_copy(c).start()
 
     high_rows, deep = wide.shape
@@ -128,9 +139,10 @@
         lax.broadcasted_iota(jnp.int32, (high_rows, parts), 0) // LC
         == lax.broadcasted_iota(jnp.int32, (high_rows, parts), 1), 1.0, 0.0,
     ).astype(jnp.bfloat16)
+    all_points = mixing.shape[1]
     spread_q = jnp.where(
-        lax.broadcasted_iota(jnp.int32, (deep // LC, deep), 1) // LC
-        == lax.broadcasted_iota(jnp.int32, (deep // LC, deep), 0), 1.0, 0.0,
+        lax.broadcasted_iota(jnp.int32, (all_points, deep), 1) // LC + line * (deep // LC)
+        == lax.broadcasted_iota(jnp.int32, (all_points, deep), 0), 1.0, 0.0,
     ).astype(jnp.bfloat16)
     tall = jnp.dot(spread_p, mixing[...], preferred_element_type=jnp.float32).astype(jnp.bfloat16)
     full = jnp.dot(tall, spread_q, preferred_element_type=jnp.float32)
@@ -171,6 +183,66 @@
                 parts, LC, width
             )
 
+    def partial_sum(c, slot):
+        block = incoming[c, :, slot].reshape(deep, rows)
+        return jnp.dot(wide[...], block, preferred_element_type=jnp.float32).reshape(parts, LC, rows)
+
+    def forward(c):
+        for slot in list(range(LINE - 1, 0, -1)):
+
+            @pl.when((line == 0) & (slot > 0))
+            def _():
+                passed[c, slot] = partial_sum(c, slot).astype(jnp.bfloat16)
+                line_copy(c, slot, slot, group).start()
+
+            @pl.when((line > 0) & (line < slot))
+            def _():
+                value = partial_sum(c, slot)
+                line_copy(c, slot, slot, group).wait_recv()
+                passed[c, slot] = (value + landed[c, slot].astype(jnp.float32)).astype(jnp.bfloat16)
+                line_copy(c, slot, slot, group).start()
+
+        for slot in range(LINE - 1):
+
+            @pl.when(line > slot)
+            def _():
+                value = partial_sum(c, slot)
+
+                @pl.when(line == LINE - 1)
+                def _():
+                    passed[c, slot] = value.astype(jnp.bfloat16)
+
+                @pl.when(line < LINE - 1)
+                def _():
+                    line_copy(c, slot, slot, -group).wait_recv()
+                    passed[c, slot] = (value + landed[c, slot].astype(jnp.float32)).astype(jnp.bfloat16)
+
+                landing = jnp.where(line - 1 == slot, LINE, slot)
+                line_copy(c, slot, landing, -group).start()
+
+    def finish(c):
+        base = partial_sum(c, line)
+
+        @pl.when(line == 0)
+        def _():
+            line_copy(c, 0, LINE, -group).wait_recv()
+            moments[:, c] = (base + landed[c, LINE].astype(jnp.float32)).astype(jnp.bfloat16)
+
+        @pl.when(line == LINE - 1)
+        def _():
+            line_copy(c, 0, LINE - 1, group).wait_recv()
+            moments[:, c] = (base + landed[c, LINE - 1].astype(jnp.float32)).astype(jnp.bfloat16)
+
+        @pl.when((line > 0) & (line < LINE - 1))
+        def _():
+            line_copy(c, 0, line, group).wait_recv()
+            line_copy(c, 0, LINE, -group).wait_recv()
+            both = landed[c, line].astype(jnp.float32) + landed[c, LINE].astype(jnp.float32)
+            moments[:, c] = (base + both).astype(jnp.bfloat16)
+
+        for copy in halo_copies(c):
+            copy.start()
+
     for c in range(chunks):
         own_copy(c).wait()
 
@@ -178,14 +250,14 @@
             copy_out(c, o).wait_recv()
             return carry
 
-        lax.fori_loop(1, quads, arrive, 0)
-        block = incoming[c].reshape(deep, rows)
-        mixed = jnp.dot(wide[...], block, preferred_element_type=jnp.float32)
-        moments[:, c] = mixed.astype(jnp.bfloat16).reshape(parts, LC, rows)
-        for copy in halo_copies(c):
-            copy.start()
+        lax.fori_loop(1, group, arrive, 0)
+        forward(c)
         if c:
-            apply_band(c - 1)
+            finish(c - 1)
+        if c > 1:
+            apply_band(c - 2)
+    finish(chunks - 1)
+    apply_band(chunks - 2)
 
     def prod(left, right):
         return lax.dot_general(left, right, NT, preferred_element_type=jnp.float32)
@@ -276,7 +348,8 @@
                 last[m, s + 1] = summed
                 row_copy(m, s + 1).start()
             else:
-                ritz[:, 2 * m * half : 2 * (m + 1) * half] = summed * scale
+                for p in range(2):
+                    ritz[:, m, p, :] = summed[:, p * half : (p + 1) * half] * scale
 
     for c in range(chunks):
 
@@ -284,9 +357,15 @@
             copy_out(c, o).wait_send()
             return carry
 
-        lax.fori_loop(1, quads, leave, 0)
+        lax.fori_loop(1, group, leave, 0)
         for copy in halo_copies(c):
             copy.wait_send()
+        for slot in range(LINE):
+
+            @pl.when(line != slot)
+            def _():
+                line_copy(c, slot, slot, group).wait_send()
+
     for m in range(2):
         for s in range(steps):
             step_copy(m, s).wait_send()
@@ -301,6 +380,7 @@
     half = KMOM * columns
     share = half // quads
     side = (band.shape[2] - band.shape[1]) // 2
+    group = quads // LINE
     steps = quads.bit_length() - 1
     row_steps = groups_r.bit_length() - 1
     bf, f4 = jnp.bfloat16, jnp.float32
@@ -309,25 +389,29 @@
         functools.partial(fused_kernel, quads, groups_r, scale),
         out_shape=(
             jax.ShapeDtypeStruct((parts, chunks, LC, rows), bf),
-            jax.ShapeDtypeStruct((share, 4 * half), f4),
+            jax.ShapeDtypeStruct((share, 2, 2, half), f4),
         ),
         in_specs=[pl.BlockSpec(memory_space=pltpu.VMEM)] * 3,
         out_specs=(pl.BlockSpec(memory_space=pltpu.VMEM),) * 2,
         scratch_shapes=[
-            pltpu.VMEM((chunks, owners, points, LC, rows), bf),
-            pltpu.VMEM((chunks, owners * points, LC, rows), bf),
+            pltpu.VMEM((chunks, group, LINE, points, LC, rows), bf),
+            pltpu.VMEM((chunks, group, LINE, points, LC, rows), bf),
+            pltpu.VMEM((chunks, LINE, parts, LC, rows), bf),
+            pltpu.VMEM((chunks, LINE + 1, parts, LC, rows), bf),
             pltpu.VMEM((parts, chunks, LC, rows), bf),
             pltpu.VMEM((parts, chunks, LC, side), bf),
             pltpu.VMEM((parts, chunks, LC, side), bf),
-            pltpu.VMEM((parts * LC, owners * points * LC), bf),
+            pltpu.VMEM((parts * LC, group * points * LC), bf),
             pltpu.VMEM((2, quads, share, 2 * half), f4),
             pltpu.VMEM((2, quads, share, 2 * half), bf),
             pltpu.VMEM((2, quads, share, 2 * half), bf),
             pltpu.VMEM((2, row_steps, share, 2 * half), f4),
             pltpu.VMEM((2, row_steps, share, 2 * half), f4),
             dma((chunks,)),
-            dma((chunks, quads)),
-            dma((chunks, quads)),
+            dma((chunks, group)),
+            dma((chunks, group)),
+            dma((chunks, LINE)),
+            dma((chunks, LINE + 1)),
             dma((2, chunks)),
             dma((2, chunks)),
             dma((2, steps)),
@@ -369,7 +453,7 @@
     applied, ritz = fused(shaped, mixing, band, quads, rows, 1.0 / (rows_dev * quads * rows))
     return (
         applied.reshape(2 * half_cols, rows_dev),
-        ritz.reshape(half_cols // quads, 2, 2, half_cols),
+        ritz,
     )
 
 

time: 180 us -> 164 us (0.911)
  Pallas kernels: 163 us -> 147 us
    pallas_call x1, Pallas kernels: 163 us -> 147 us  [fused(): pl.pallas_call(functools.partial(fused_kernel, quads, groups_r, scale), o...]
    reshape x1 -> x0, local copies, waits for them, and re-layouts: 1.87 us -> none  [per_device(): ritz.reshape(half_cols // quads, 2, 2, half_cols)]
where the time goes in v3:
time: 164 us; the launch traced here: 162 us
  Pallas kernels  147 us (90%)
  local copies, waits for them, and re-layouts  10.6 us (6%)
  other arithmetic  4.18 us (3%)
    pallas_call x1, Pallas kernels, fused(): pl.pallas_call(functools.partial(fused_kernel, quads, groups_r, scale), o...  147 us
    convert_element_type x48, local copies, waits for them, and re-layouts, band_blocks(): hit = (local[:, :, n] == d).astype(jnp.float32)[:, :, None, None]  4.42 us

profile of v3, /device:TPU:0, one launch (start us, length us, event | category | flops | bytes accessed | tf_op | source)
XLA Modules:
  0.0 162.5 jit_solution(13477190324785061981)
XLA Ops:
  0.7 0.8 slice_bitcast_fusion.1
  1.4 0.7 subtract_add_fusion
  2.2 0.1 copy.304
  2.3 0.7 negate_convert_fusion
  3.1 0.1 copy.352
  3.2 0.1 copy.344
  3.3 0.1 copy.312
  3.3 0.1 copy.311
  3.4 0.1 copy.310
  3.5 0.1 copy.309
  4.0 0.1 copy.348
  4.5 0.1 copy.349
  4.7 0.1 copy.326
  5.1 0.1 copy.327
  5.3 0.1 copy.343
  5.8 0.1 copy.345
  6.2 0.1 copy.314
  6.4 0.1 copy.330
  6.9 0.1 copy.331
  7.3 0.1 copy.332
  7.5 0.1 copy.302
  7.7 0.7 copy.353.mixing
  8.4 0.5 fusion.39
  8.9 0.5 fusion.31
  9.3 0.5 fusion.23
  9.8 0.5 fusion.15
  10.3 0.5 fusion.47
  10.7 0.5 fusion.7
  11.2 1.1 concatenate.3
  12.3 146.9 %shard_map.68 = (bf16[16,4,16,640]{3,2,1,0:T(8,128)(2,1)}, f32[32,2,2,512]{3,2,1,0:T(2,128)}) custom-call(bf16[4,64,16,640]{3,2,1,0:T(8,128)(2,1)} %bitcast.116, bf16[16,64]{1,0:T(8,128)(2,1)} %copy.353.mixing, bf16[5,128,384]{2,1,0:T(8,128)(2,1)} %bitcast.117), custom_call_target="tpu_custom_call" | custom-call | tf_op jit(solution)/shard_map/pallas_call | solution.py:388
  159.2 2.5 %copy.356 = bf16[1024,640]{1,0:T(8,128)(2,1)} copy(bf16[1024,640]{1,0:T(8,128)(2,1)} %bitcast.118) | data formatting | bytes 2621440
  161.8 0.7 copy.357
  (46 shorter events, 3.2 us)
Async XLA Ops:
  0.6 7.8 %copy-start = (bf16[10,64,512]{2,1,0:T(8,128)(2,1)S(1)}, bf16[10,64,512]{2,1,0:T(8,128)(2,1)}, u32[]{:S(2)}) copy-start(bf16[10,64,512]{2,1,0:T(8,128)(2,1)} %param.9) | copy-start | bytes 1966084
  159.2 2.5 %copy-start.1 = (f32[32,2,2,512]{3,2,1,0:T(2,128)S(1)}, f32[32,2,2,512]{3,2,1,0:T(2,128)}, u32[]{:S(2)}) copy-start(f32[32,2,2,512]{3,2,1,0:T(2,128)} %get-tuple-element.64) | copy-start | bytes 786436

commit v4 on v3

--- a/solution.py
+++ b/solution.py
@@ -40,8 +40,8 @@
 
 
 def fused_kernel(
-    quads, groups_r, scale, solutions, mixing, band, applied, ritz,
-    outgoing, incoming, passed, landed, moments, low, high, wide, gram, sent, got, last, last_got,
+    quads, groups_r, scale, solutions, mixing, neighbours, hblocks, applied, ritz,
+    band, outgoing, incoming, passed, landed, moments, low, high, wide, gram, sent, got, last, last_got,
     own_sem, a2a_send, a2a_recv, line_send, line_recv, halo_send, halo_recv, step_send, step_recv, row_send, row_recv,
 ):
     points, columns, owners, rows = solutions.shape
@@ -49,7 +49,8 @@
     parts = 2 * KMOM
     half = KMOM * columns
     share = half // quads
-    pairs, width, reach = band.shape
+    cells, orbitals, reach = band.shape
+    pairs, width = cells // 2, 2 * orbitals
     side = low.shape[-1]
     me = lax.axis_index("quad")
     row = lax.axis_index("rows")
@@ -151,6 +152,25 @@
     )
     wide[...] = jnp.where(same, full, 0.0).astype(jnp.bfloat16)
 
+    first_cell = flat * cells
+
+    def pack_cell(cell, carry):
+        base = first_cell - HALO + cell // 2 * 2
+        blocks = [
+            hblocks[cell, :, n * orbitals : (n + 1) * orbitals].astype(jnp.float32) for n in range(NB)
+        ]
+        places = [neighbours[cell, n] - base for n in range(NB)]
+        chosen = []
+        for d in range(2 * HALO + 2):
+            summed = jnp.zeros((orbitals, orbitals), jnp.float32)
+            for n in range(NB):
+                summed = summed + jnp.where(places[n] == d, 1.0, 0.0) * blocks[n]
+            chosen.append(summed)
+        band[cell] = jnp.concatenate(chosen, -1).astype(jnp.bfloat16)
+        return carry
+
+    lax.fori_loop(0, cells, pack_cell, 0)
+
     def halo_copies(c):
         up = pltpu.make_async_remote_copy(
             src_ref=moments.at[:, c, :, rows - side : rows],
@@ -177,7 +197,7 @@
         near = near.reshape(parts * LC, rows + 2 * side)
         for i in range(pairs):
             out = lax.dot_general(
-                near[:, i * width : i * width + reach], band[i], NT, preferred_element_type=jnp.float32
+                near[:, i * width : i * width + reach], band[2 * i : 2 * i + 2].reshape(width, reach), NT, preferred_element_type=jnp.float32
             )
             applied[:, c, :, i * width : (i + 1) * width] = out.astype(jnp.bfloat16).reshape(
                 parts, LC, width
@@ -373,13 +393,14 @@
             row_copy(m, s).wait_send()
 
 
-def fused(solutions, mixing, band, quads, groups_r, scale):
+def fused(solutions, mixing, neighbours, hblocks, quads, groups_r, scale):
     points, columns, owners, rows = solutions.shape
     chunks = columns // LC
     parts = 2 * KMOM
     half = KMOM * columns
     share = half // quads
-    side = (band.shape[2] - band.shape[1]) // 2
+    cells, orbitals, _ = hblocks.shape
+    side = HALO * orbitals
     group = quads // LINE
     steps = quads.bit_length() - 1
     row_steps = groups_r.bit_length() - 1
@@ -391,9 +412,15 @@
             jax.ShapeDtypeStruct((parts, chunks, LC, rows), bf),
             jax.ShapeDtypeStruct((share, 2, 2, half), f4),
         ),
-        in_specs=[pl.BlockSpec(memory_space=pltpu.VMEM)] * 3,
+        in_specs=[
+            pl.BlockSpec(memory_space=pltpu.VMEM),
+            pl.BlockSpec(memory_space=pltpu.VMEM),
+            pl.BlockSpec(memory_space=pltpu.SMEM),
+            pl.BlockSpec(memory_space=pltpu.VMEM),
+        ],
         out_specs=(pl.BlockSpec(memory_space=pltpu.VMEM),) * 2,
         scratch_shapes=[
+            pltpu.VMEM((cells, orbitals, (2 * HALO + 2) * orbitals), bf),
             pltpu.VMEM((chunks, group, LINE, points, LC, rows), bf),
             pltpu.VMEM((chunks, group, LINE, points, LC, rows), bf),
             pltpu.VMEM((chunks, LINE, parts, LC, rows), bf),
@@ -422,35 +449,16 @@
         compiler_params=pltpu.CompilerParams(
             collective_id=0, has_side_effects=True, vmem_limit_bytes=56 * 2**20
         ),
-    )(solutions, mixing, band)
-
-
-def band_blocks(neighbours, hblocks, first_cell):
-    cells, orbitals, _ = hblocks.shape
-    pairs = cells // 2
-    window = 2 * HALO + 2
-    local = (neighbours - first_cell + HALO).reshape(pairs, 2, NB) - 2 * jnp.arange(pairs)[:, None, None]
-    split = hblocks.reshape(pairs, 2, orbitals, NB * orbitals)
-    chosen = []
-    for d in range(window):
-        total = 0.0
-        for n in range(NB):
-            hit = (local[:, :, n] == d).astype(jnp.float32)[:, :, None, None]
-            total += hit * split[:, :, :, n * orbitals : (n + 1) * orbitals].astype(jnp.float32)
-        chosen.append(total.astype(jnp.bfloat16))
-    return jnp.concatenate(chosen, -1).reshape(pairs, 2 * orbitals, window * orbitals)
+    )(solutions, mixing, neighbours, hblocks)
 
 
 def per_device(solutions, angles, qweights, neighbours, hblocks):
     quads, rows = lax.axis_size("quad"), lax.axis_size("rows")
     rows_dev = solutions.shape[4]
-    cells_dev = hblocks.shape[0]
     half_cols = KMOM * LCOL
     mixing = moment_coefficients(angles, qweights)
-    first_cell = (lax.axis_index("quad") * rows + lax.axis_index("rows")) * cells_dev
-    band = band_blocks(neighbours, hblocks, first_cell)
     shaped = solutions.reshape((-1,) + solutions.shape[2:])
-    applied, ritz = fused(shaped, mixing, band, quads, rows, 1.0 / (rows_dev * quads * rows))
+    applied, ritz = fused(shaped, mixing, neighbours, hblocks, quads, rows, 1.0 / (rows_dev * quads * rows))
     return (
         applied.reshape(2 * half_cols, rows_dev),
         ritz,

time: 164 us -> 156 us (0.951)
  local copies, waits for them, and re-layouts: 10.6 us -> 6.21 us
  other arithmetic: 4.18 us -> 0.72 us
    convert_element_type x48 -> x0, local copies, waits for them, and re-layouts: 4.42 us -> none  [band_blocks(): hit = (local[:, :, n] == d).astype(jnp.float32)[:, :, None, None]]
    convert_element_type x9 -> x0, other arithmetic: 2.76 us -> none  [the longest x6 2.73 us: band_blocks(): chosen.append(total.astype(jnp.bfloat16))]
    unnamed x6 -> x5, local copies, waits for them, and re-layouts: 3.24 us -> 4.6 us
where the time goes in v4:
time: 156 us; the launch traced here: 154 us
  Pallas kernels  147 us (94%)
  local copies, waits for them, and re-layouts  6.21 us (4%)
    pallas_call x1, Pallas kernels, fused(): pl.pallas_call(functools.partial(fused_kernel, quads, groups_r, scale), o...  147 us
    unnamed x5, local copies, waits for them, and re-layouts  4.6 us

profile of v4, /device:TPU:0, one launch (start us, length us, event | category | flops | bytes accessed | tf_op | source)
XLA Modules:
  0.0 154.3 jit_solution(14372124182277020968)
XLA Ops:
  0.6 0.8 slice_bitcast_fusion.1
  1.4 0.7 negate_convert_fusion
  2.1 1.4 copy.13.neighbours
  3.5 0.1 copy.11
  3.6 0.1 convert_element_type.3
  3.7 0.7 copy.12.mixing
  4.4 146.7 %shard_map.68 = (bf16[16,4,16,640]{3,2,1,0:T(8,128)(2,1)}, f32[32,2,2,512]{3,2,1,0:T(2,128)}) custom-call(bf16[4,64,16,640]{3,2,1,0:T(8,128)(2,1)} %bitcast.12, bf16[16,64]{1,0:T(8,128)(2,1)} %copy.12.mixing, s32[10,8]{1,0:T(8,128)} %copy.13.neighbours, bf16[10,64,512]{2,1,0:T(8,128)(2,1)} %hblocks.1), custom_call_target="tpu_custom_call" | custom-call | tf_op jit(solution)/shard_map/pallas_call | solution.py:409
  151.1 0.0 copy-start
  151.1 2.5 %copy.16 = bf16[1024,640]{1,0:T(8,128)(2,1)} copy(bf16[1024,640]{1,0:T(8,128)(2,1)} %bitcast.13) | data formatting | bytes 2621440
  153.6 0.0 copy-done
  153.6 0.7 copy.17
  (2 shorter events, 0.0 us)
Async XLA Ops:
  151.1 2.5 %copy-start = (f32[32,2,2,512]{3,2,1,0:T(2,128)S(1)}, f32[32,2,2,512]{3,2,1,0:T(2,128)}, u32[]{:S(2)}) copy-start(f32[32,2,2,512]{3,2,1,0:T(2,128)} %get-tuple-element.16) | copy-start | bytes 786436
